TPU v7x, 32 devices: a whole 2x2x4 slice. The times are simulated.
32 devices in a mesh: groups: 2 (over x), tm: 2 (over core), slab: 8 (over z, y).
Axes of the slice: x: 2, y: 2, z: 4, core: 2. Of those that a mesh axis runs over, the one named last changes fastest.
Arguments:
- window_states: float32 [8, 64, 16, 512], P('tm', ('groups', 'slab')), parts along dimension 1, may hold values from -6 to 6
- spatial_weight: bfloat16 [320, 144], replicated, may hold values from -0.5 to 0.5
- temporal_weight: bfloat16 [3, 320, 320], replicated, may hold values from -0.1875 to 0.1875
- out_weight: bfloat16 [16, 320], replicated, may hold values from -0.3125 to 0.3125
- time_embed: float32 [1000, 320], replicated, may hold values from -6 to 6
- step_size: float32 [1000], replicated, may hold values from 0.1 to 0.4
- time_index: int32 [48], P('groups'), parts along dimension 0, may hold values from 0 to 999
- slides: int32 [4], P('groups'), parts along dimension 0, may hold values from 1 to 7
Outputs:
- final_states: float32 [8, 64, 16, 512], P('tm', ('groups', 'slab')), parts along dimension 1
There are 2 independent parts, one for each index of `groups`. A program takes and returns all parts, laid end to end along the dimension named above; an argument that names none is the same for every part. Nothing has to cross between parts.
All inputs are finite; a program needn't handle non-finite values.
Results may differ from a plain program's by a relative error of at most 0.002.
Values may be sent and summed in bfloat16 or wider, within the bound.
A program may use at most 128 MiB of HBM per device.

v0:
```python
import jax
import jax.numpy as jnp
from jax import lax
from jax.sharding import PartitionSpec as P

C = 16
HEIGHT = 16
WIDTH = 32
ITERS = 2


def with_halo(cells, sides, width):
    for axis, dim in sides:
        count = lax.axis_size(axis)
        ends = count - 1
        head = lax.slice_in_dim(cells, 0, width, axis=dim)
        tail = lax.slice_in_dim(cells, cells.shape[dim] - width, cells.shape[dim], axis=dim)
        cells = jnp.concatenate(
            [
                lax.ppermute(tail, axis, [(i, (i + 1) % count) for i in range(ends)]),
                cells,
                lax.ppermute(head, axis, [((i + 1) % count, i) for i in range(ends)]),
            ],
            axis=dim,
        )
    return cells


def carried_in(part, axis, combine, identity):
    place = lax.axis_index(axis)
    gathered = lax.all_gather(part, axis)
    state = jnp.zeros_like(part) + jnp.asarray(identity, part.dtype)

    def one(lap, state):
        return combine(state, lax.dynamic_index_in_dim(gathered, lap, 0, False))

    return lax.fori_loop(0, place, one, state)


def shift_table():
    cells = HEIGHT * WIDTH
    target = jnp.arange(cells, dtype=jnp.int32)
    cell_row = target // WIDTH
    cell_col = target % WIDTH
    source_ids = jnp.arange(cells, dtype=jnp.int32)
    tables = []
    for row_shift in range(3):
        for col_shift in range(3):
            src_row = cell_row + row_shift - 1
            src_col = cell_col + col_shift - 1
            valid_cells = (src_row >= 0) & (src_row < HEIGHT) & (src_col >= 0) & (src_col < WIDTH)
            source = src_row * WIDTH + src_col
            picked = (source_ids[:, None] == source[None, :]) & valid_cells[None, :]
            tables.append(picked)
    return jnp.stack(tables, axis=0).astype(jnp.bfloat16)


def spatial(latent, spatial_weight):
    times, frames = (latent.shape[0], latent.shape[1])
    moved = jnp.einsum("tfcp,spq->tfscq", latent, shift_table(), preferred_element_type=jnp.float32)
    columns = moved.astype(jnp.bfloat16).reshape(times, frames, 9 * C, HEIGHT * WIDTH)
    return jnp.einsum("oc,tfcp->tfop", spatial_weight, columns, preferred_element_type=jnp.float32)


def add_states(earlier, later):
    return earlier + later


def local(
    window_states,
    spatial_weight,
    temporal_weight,
    out_weight,
    time_embed,
    step_size,
    time_index,
    slides,
):
    states = window_states
    local_times = states.shape[0]
    local_frames = states.shape[1]
    time_rank = lax.axis_index("tm")
    time_count = lax.axis_size("tm")
    slab_rank = lax.axis_index("slab")
    slab_count = lax.axis_size("slab")
    offset = jnp.zeros((), jnp.int32)
    for sweep in range(ITERS):
        indices = lax.dynamic_slice_in_dim(
            time_index, offset + time_rank * local_times, local_times
        )
        one_hot = (
            indices[:, None] == jnp.arange(time_embed.shape[0], dtype=jnp.int32)[None, :]
        ).astype(jnp.float32)
        embed = jnp.dot(one_hot, time_embed, precision=lax.Precision.HIGHEST)
        deltas = jnp.dot(one_hot, step_size, precision=lax.Precision.HIGHEST)
        latent = states.astype(jnp.bfloat16)
        widened = with_halo(latent, (("slab", 1),), 1)
        pre = spatial(widened, spatial_weight) + embed[:, None, :, None]
        first = jax.nn.silu(pre).astype(jnp.bfloat16)
        global_frame = slab_rank * local_frames - 1 + jnp.arange(local_frames + 2, dtype=jnp.int32)
        inside = (global_frame >= 0) & (global_frame < local_frames * slab_count)
        framed = jnp.where(inside[None, :, None, None], first, jnp.zeros_like(first))
        middle = jnp.einsum(
            "oc,tfcp->tfop",
            temporal_weight[0],
            framed[:, 0:local_frames],
            preferred_element_type=jnp.float32,
        )
        for lagged in range(1, 3):
            middle = middle + jnp.einsum(
                "oc,tfcp->tfop",
                temporal_weight[lagged],
                framed[:, lagged : lagged + local_frames],
                preferred_element_type=jnp.float32,
            )
        second = jax.nn.silu(middle).astype(jnp.bfloat16)
        drifts = jnp.einsum("ch,tfhp->tfcp", out_weight, second, preferred_element_type=jnp.float32)
        weighted = deltas[:, None, None, None] * drifts
        running = jnp.cumsum(weighted, axis=0)
        summed = running[-1]
        first_state = jnp.where(time_rank == 0, states[0], jnp.zeros_like(states[0]))
        handed = summed + first_state
        carried = carried_in(handed, "tm", add_states, jnp.zeros_like(handed))
        anchor = jnp.where(time_rank == 0, states[0], carried)
        updated = anchor[None] + (running - weighted)
        ending = anchor + summed
        whole, tails = (
            lax.all_gather(updated, "tm", axis=0, tiled=True),
            lax.all_gather(ending[None], "tm", axis=0, tiled=True),
        )
        tail = tails[time_count - 1]
        extended = jnp.concatenate([whole, jnp.broadcast_to(tail[None], whole.shape)], axis=0)
        shift_now = slides[sweep]
        states = lax.dynamic_slice_in_dim(
            extended, shift_now + time_rank * local_times, local_times
        )
        offset = offset + shift_now
    return states


def solution(mesh):
    return jax.shard_map(
        local,
        mesh=mesh,
        in_specs=(
            P("tm", ("groups", "slab"), None, None),
            P(),
            P(),
            P(),
            P(),
            P(),
            P("groups"),
            P("groups"),
        ),
        out_specs=P("tm", ("groups", "slab"), None, None),
        check_vma=False,
    )
```

profile of v0, /device:TPU:0, one launch (start us, length us, event | category | flops | bytes accessed | tf_op | source)
XLA Modules:
  0.0 149.2 jit_solution(11588758929160838910)
XLA Ops:
  6.5 0.0 copy-start
  6.5 1.2 convert_element_type.34
  7.7 4.9 %collective-permute-start = (bf16[4,1,16,512]{3,2,1,0:T(8,128)(2,1)S(1)}, bf16[4,1,16,512]{3,2,1,0:T(8,128)(2,1)S(1)}, u32[]{:S(2)}, u32[]{:S(2)}) collective-permute-start(bf16[4,1,16,512]{3,2,1,0:T(8,128)(2,1)S(1)} %get-tuple-element.77), channel_id=1, source_target_pairs={{0,1},{1,2},{2,3},{3,4},{4,5},{5,6},{6,7},{8,9},{9,10},{10,11},{11... | collective-permute-start | bytes 196616 | tf_op jit(solution)/shard_map/ppermute | solution.py:20
  12.6 1.3 collective-permute-start.1
  13.9 1.4 fusion.155
  16.2 0.8 fusion.154
  17.0 0.6 fusion.115
  17.7 0.9 convolution_bitcast_fusion.1
  18.6 0.9 fusion.69
  19.5 0.9 fusion.71
  20.4 0.9 fusion.73
  21.4 0.9 fusion.75
  22.3 0.9 fusion.77
  23.2 0.9 fusion.79
  24.1 0.9 fusion.81
  25.0 0.9 fusion.83
  25.9 0.9 fusion.85
  26.7 0.0 collective-permute-done
  26.7 0.0 collective-permute-done.1
  26.8 3.7 %convert_bitcast_fusion.1 = bf16[4,6,9,16,512]{4,3,1,0,2:T(8,128)(2,1)S(1)} fusion(pred[9,512,512]{2,1,0:T(8,128)(4,1)} %fusion.85, bf16[4,1,16,512]{3,2,1,0:T(8,128)(2,1)S(1)} %collective-permute-done.1, bf16[4,4,16,512]{3,2,1,0:T(8,128)(2,1)S(1)} %convert_element_type.34, bf16[4,1,16,512]{3,2,1,0:T(8,128)(2,1)S(1)} %collective-permute-done), kind=kOutput, calls=%fused_computation.47 | convolution fusion | flops 1814888448 | bytes 6291456 | tf_op jit(solution)/shard_map/tfcp,spq->tfscq/dot_general | solution.py:60
  30.5 0.0 copy-start.5
  30.5 0.4 copy.11
  30.9 0.5 copy-done.5
  31.4 5.9 %broadcast_select_fusion.1 = bf16[4,6,320,512]{3,2,1,0:T(8,128)(2,1)S(1)} fusion(pred[6]{0:T(512)(128)(4,1)S(1)} %compare_and_fusion.2, f32[4,320]{1,0:T(4,128)S(1)} %fusion.115, bf16[4,6,144,512]{3,2,1,0:T(8,128)(2,1)S(1)} %bitcast.171, bf16[320,144]{0,1:T(8,128)(2,1)S(1)} %copy-done.5), kind=kOutput, calls=%fused_computation.31 | convolution fusion | flops 1159987200 | bytes 11500550 | tf_op jit(solution)/shard_map/oc,tfcp->tfop/dot_general | solution.py:62
  37.3 6.2 %fusion.26 = f32[4,4,512,320]{2,3,1,0:T(8,128)} fusion(bf16[4,6,320,512]{3,2,1,0:T(8,128)(2,1)S(1)} %broadcast_select_fusion.1, bf16[3,320,320]{2,1,0:T(8,128)(2,1)S(1)} %copy-done.4), kind=kOutput, calls=%fused_computation.38 | convolution fusion | flops 1677721600 | bytes 15974400 | tf_op jit(solution)/shard_map/oc,tfcp->tfop/dot_general | solution.py:110
  43.5 0.2 copy-done.3
  43.7 5.5 %fusion.28 = f32[4,4,512,320]{2,3,1,0:T(8,128)} fusion(bf16[4,6,320,512]{3,2,1,0:T(8,128)(2,1)S(1)} %broadcast_select_fusion.1, bf16[3,320,320]{2,1,0:T(8,128)(2,1)S(1)} %copy-done.4), kind=kOutput, calls=%fused_computation.40 | convolution fusion | flops 1677721600 | bytes 15974400 | tf_op jit(solution)/shard_map/oc,tfcp->tfop/dot_general | solution.py:110
  49.1 10.8 %fusion.53 = f32[4,4,16,512]{3,2,1,0:T(8,128)S(1)} fusion(f32[4,4,512,320]{2,3,1,0:T(8,128)} %fusion.26, f32[4,4,512,320]{2,3,1,0:T(8,128)} %fusion.28, bf16[4,6,320,512]{3,2,1,0:T(8,128)(2,1)} %copy-done.3, f32[4]{0:T(128)S(1)} %convolution_bitcast_fusion.1, bf16[3,320,320]{2,1,0:T(8,128)(2,1)S(1)} %copy-done.4, bf16[16,320]{1,0:T(8,128)(2,1)S(1)} %copy-done.7), kind=kOutput, calls=%fused_computation.53 | convolution fusion | flops 1780088832 | bytes 26997248 | tf_op jit(solution)/shard_map/ch,tfhp->tfcp/dot_general | solution.py:117
  59.9 2.0 %fusion.156 = f32[4,4,16,512]{3,2,1,0:T(8,128)S(1)} fusion(f32[4,4,16,512]{3,2,1,0:T(8,128)S(1)} %fusion.53), kind=kOutput, calls=%fused_computation.184 | output fusion | flops 393216 | bytes 1048576 | tf_op jit(solution)/shard_map/jit(cumsum)/reduce_window_sum | solution.py:119
  61.9 0.9 select_add_fusion.1
  62.8 2.0 %all_gather.20 = f32[2,4,16,512]{3,2,1,0:T(8,128)S(1)} all-gather(f32[1,4,16,512]{3,2,1,0:T(8,128)S(1)} %select_add_fusion.1), channel_id=1, replica_groups=mesh['groups'=2,'tm'=2,'slab'=8] {'tm'}, dimensions={0}, use_global_device_ids=true | all-gather | bytes 393216 | tf_op jit(solution)/shard_map/all_gather | solution.py:31
  64.8 0.9 bitcast_add_fusion.3
  65.8 0.9 subtract_add_fusion.1
  66.7 0.0 all-gather.5.cloned.1.call-update
  66.7 0.0 all-gather.7.cloned.1.call-start
  66.8 0.6 fusion.114
  67.4 2.0 %all-gather = f32[8,16,512]{2,1,0:T(8,128)S(1)} all-gather(f32[4,16,512]{2,1,0:T(8,128)S(1)} %get-tuple-element.73), channel_id=2, replica_groups=mesh['groups'=2,'tm'=2,'slab'=8] {'tm'}, dimensions={0}, use_global_device_ids=true | all-gather | bytes 393216 | tf_op jit(solution)/shard_map/all_gather | solution.py:129
  69.5 8.8 %all-gather.5.cloned.1.call-done = f32[8,4,16,512]{3,2,1,0:T(8,128)} async-done(((f32[4,4,16,512]{3,2,1,0:T(8,128)}), f32[8,4,16,512]{3,2,1,0:T(8,128)}) %all-gather.5.cloned.1.call-update) | async-done | bytes 1048592 | tf_op jit(solution)/shard_map/all_gather | solution.py:128
  78.3 0.1 broadcast_in_dim.23
  78.4 1.9 %fusion.150 = (bf16[4,4,16,512]{3,2,1,0:T(8,128)(2,1)S(1)}, f32[4,4,16,512]{3,2,1,0:T(8,128)}) fusion(s32[]{:T(128)S(6)} %select_n.215, f32[8,4,16,512]{3,2,1,0:T(8,128)S(1)} %broadcast_in_dim.23, f32[8,4,16,512]{3,2,1,0:T(8,128)} %all-gather.5.cloned.1.call-done), kind=kLoop, calls=%fused_computation.179 | loop fusion | flops 262144 | bytes 2883588 | tf_op jit(solution)/shard_map/convert_element_type | solution.py:96
  80.3 3.6 %collective-permute-start.2 = (bf16[4,1,16,512]{3,2,1,0:T(8,128)(2,1)S(1)}, bf16[4,1,16,512]{3,2,1,0:T(8,128)(2,1)S(1)}, u32[]{:S(2)}, u32[]{:S(2)}) collective-permute-start(bf16[4,1,16,512]{3,2,1,0:T(8,128)(2,1)S(1)} %get-tuple-element.75), channel_id=1, source_target_pairs={{0,1},{1,2},{2,3},{3,4},{4,5},{5,6},{6,7},{8,9},{9,10},{10,11},{11... | collective-permute-start | bytes 196616 | tf_op jit(solution)/shard_map/ppermute | solution.py:20
  84.0 1.3 collective-permute-start.3
  85.3 0.2 convolution_bitcast_fusion
  85.4 0.4 collective-permute-done.2
  85.8 4.3 %collective-permute-done.3 = bf16[4,1,16,512]{3,2,1,0:T(8,128)(2,1)S(1)} collective-permute-done((bf16[4,1,16,512]{3,2,1,0:T(8,128)(2,1)S(1)}, bf16[4,1,16,512]{3,2,1,0:T(8,128)(2,1)S(1)}, u32[]{:S(2)}, u32[]{:S(2)}) %collective-permute-start.3) | collective-permute-done | bytes 65568 | tf_op jit(solution)/shard_map/ppermute | solution.py:22
  90.1 3.7 %convert_bitcast_fusion = bf16[4,6,9,16,512]{4,3,1,0,2:T(8,128)(2,1)S(1)} fusion(pred[9,512,512]{2,1,0:T(8,128)(4,1)} %fusion.85, bf16[4,1,16,512]{3,2,1,0:T(8,128)(2,1)S(1)} %collective-permute-done.3, bf16[4,4,16,512]{3,2,1,0:T(8,128)(2,1)S(1)} %get-tuple-element.71, bf16[4,1,16,512]{3,2,1,0:T(8,128)(2,1)S(1)} %collective-permute-done.2), kind=kOutput, calls=%fused_computation.46 | convolution fusion | flops 1814888448 | bytes 6291456 | tf_op jit(solution)/shard_map/tfcp,spq->tfscq/dot_general | solution.py:60
  93.8 0.0 copy-start.6
  93.9 0.4 copy.12
  94.2 0.5 copy-done.6
  94.7 5.9 %broadcast_select_fusion = bf16[4,6,320,512]{3,2,1,0:T(8,128)(2,1)S(1)} fusion(pred[6]{0:T(512)(128)(4,1)S(1)} %compare_and_fusion.2, f32[4,320]{1,0:T(4,128)S(1)} %fusion.114, bf16[4,6,144,512]{3,2,1,0:T(8,128)(2,1)S(1)} %bitcast.170, bf16[320,144]{0,1:T(8,128)(2,1)S(1)} %copy-done.6), kind=kOutput, calls=%fused_computation.30 | convolution fusion | flops 1159987200 | bytes 11500550 | tf_op jit(solution)/shard_map/oc,tfcp->tfop/dot_general | solution.py:62
  100.6 6.2 %fusion.20 = f32[4,4,512,320]{2,3,1,0:T(8,128)} fusion(bf16[4,6,320,512]{3,2,1,0:T(8,128)(2,1)S(1)} %broadcast_select_fusion, bf16[3,320,320]{2,1,0:T(8,128)(2,1)S(1)} %copy-done.4), kind=kOutput, calls=%fused_computation.32 | convolution fusion | flops 1677721600 | bytes 15974400 | tf_op jit(solution)/shard_map/oc,tfcp->tfop/dot_general | solution.py:110
  106.8 0.2 copy-done.2
  107.0 5.5 %fusion.22 = f32[4,4,512,320]{2,3,1,0:T(8,128)} fusion(bf16[4,6,320,512]{3,2,1,0:T(8,128)(2,1)S(1)} %broadcast_select_fusion, bf16[3,320,320]{2,1,0:T(8,128)(2,1)S(1)} %copy-done.4), kind=kOutput, calls=%fused_computation.34 | convolution fusion | flops 1677721600 | bytes 15974400 | tf_op jit(solution)/shard_map/oc,tfcp->tfop/dot_general | solution.py:110
  112.5 10.9 %fusion.63 = f32[4,4,16,512]{3,2,1,0:T(8,128)S(1)} fusion(f32[4,4,512,320]{2,3,1,0:T(8,128)} %fusion.20, f32[4,4,512,320]{2,3,1,0:T(8,128)} %fusion.22, bf16[4,6,320,512]{3,2,1,0:T(8,128)(2,1)} %copy-done.2, f32[4]{0:T(128)S(1)} %convolution_bitcast_fusion, bf16[3,320,320]{2,1,0:T(8,128)(2,1)S(1)} %copy-done.4, bf16[16,320]{1,0:T(8,128)(2,1)S(1)} %copy-done.7), kind=kOutput, calls=%fused_computation.55 | convolution fusion | flops 1780088832 | bytes 26997248 | tf_op jit(solution)/shard_map/ch,tfhp->tfcp/dot_general | solution.py:117
  123.3 2.0 %fusion.157 = f32[4,4,16,512]{3,2,1,0:T(8,128)S(1)} fusion(f32[4,4,16,512]{3,2,1,0:T(8,128)S(1)} %fusion.63), kind=kOutput, calls=%fused_computation.185 | output fusion | flops 393216 | bytes 1048576 | tf_op jit(solution)/shard_map/jit(cumsum)/reduce_window_sum | solution.py:119
  125.3 0.9 select_add_fusion
  126.2 2.0 %all_gather.23 = f32[2,4,16,512]{3,2,1,0:T(8,128)S(1)} all-gather(f32[1,4,16,512]{3,2,1,0:T(8,128)S(1)} %select_add_fusion), channel_id=1, replica_groups=mesh['groups'=2,'tm'=2,'slab'=8] {'tm'}, dimensions={0}, use_global_device_ids=true | all-gather | bytes 393216 | tf_op jit(solution)/shard_map/all_gather | solution.py:31
  128.3 0.9 bitcast_add_fusion.2
  129.2 0.9 subtract_add_fusion
  130.1 0.0 all-gather.7.cloned.1.call-update
  130.8 2.0 %all-gather.1 = f32[8,16,512]{2,1,0:T(8,128)S(1)} all-gather(f32[4,16,512]{2,1,0:T(8,128)S(1)} %get-tuple-element.69), channel_id=3, replica_groups=mesh['groups'=2,'tm'=2,'slab'=8] {'tm'}, dimensions={0}, use_global_device_ids=true | all-gather | bytes 393216 | tf_op jit(solution)/shard_map/all_gather | solution.py:129
  132.8 7.5 %all-gather.7.cloned.1.call-done = f32[8,4,16,512]{3,2,1,0:T(8,128)} async-done(((f32[4,4,16,512]{3,2,1,0:T(8,128)}), f32[8,4,16,512]{3,2,1,0:T(8,128)}) %all-gather.7.cloned.1.call-update) | async-done | bytes 1048592 | tf_op jit(solution)/shard_map/all_gather | solution.py:128
  140.3 0.1 broadcast_in_dim.26
  140.4 1.9 %fusion.86 = f32[4,4,16,512]{3,2,1,0:T(8,128)} fusion(s32[]{:T(128)S(6)} %select_n.220, f32[8,4,16,512]{3,2,1,0:T(8,128)} %all-gather.7.cloned.1.call-done, f32[8,4,16,512]{3,2,1,0:T(8,128)S(1)} %broadcast_in_dim.26), kind=kLoop, calls=%fused_computation.85 | loop fusion | flops 131072 | bytes 2621444 | tf_op jit(solution)/shard_map/concatenate | solution.py:132
  (39 shorter events, 0.3 us)
Async XLA Ops:
  6.5 10.5 %copy-start = (f32[1000,320]{0,1:T(8,128)S(1)}, f32[1000,320]{0,1:T(8,128)}, u32[]{:S(2)}) copy-start(f32[1000,320]{0,1:T(8,128)} %param.16) | copy-start | bytes 3840004
  6.5 71.8 %all-gather.5.cloned.1.call-start = ((), (), s32[]{:S(2)}) async-start(), calls=%async_computation | async-start | bytes 1572864 | tf_op jit(solution)/shard_map/all_gather | solution.py:128
  7.7 19.0 %collective-permute-start = (bf16[4,1,16,512]{3,2,1,0:T(8,128)(2,1)S(1)}, bf16[4,1,16,512]{3,2,1,0:T(8,128)(2,1)S(1)}, u32[]{:S(2)}, u32[]{:S(2)}) collective-permute-start(bf16[4,1,16,512]{3,2,1,0:T(8,128)(2,1)S(1)} %get-tuple-element.77), channel_id=1, source_target_pairs={{0,1},{1,2},{2,3},{3,4},{4,5},{5,6},{6,7},{8,9},{9,10},{10,11},{11... | collective-permute-start | bytes 196616 | tf_op jit(solution)/shard_map/ppermute | solution.py:20
  12.6 14.1 %collective-permute-start.1 = (bf16[4,1,16,512]{3,2,1,0:T(8,128)(2,1)S(1)}, bf16[4,1,16,512]{3,2,1,0:T(8,128)(2,1)S(1)}, u32[]{:S(2)}, u32[]{:S(2)}) collective-permute-start(bf16[4,1,16,512]{3,2,1,0:T(8,128)(2,1)S(1)} %get-tuple-element.78), channel_id=1, source_target_pairs={{1,0},{2,1},{3,2},{4,3},{5,4},{6,5},{7,6},{9,8},{10,9},{11,10},{12... | collective-permute-start | bytes 196616 | tf_op jit(solution)/shard_map/ppermute | solution.py:22
  30.5 0.9 copy-start.5
  31.4 5.9 %copy-start.4 = (bf16[3,320,320]{2,1,0:T(8,128)(2,1)S(1)}, bf16[3,320,320]{2,1,0:T(8,128)(2,1)}, u32[]{:S(2)}) copy-start(bf16[3,320,320]{2,1,0:T(8,128)(2,1)} %param.14) | copy-start | bytes 1843204
  37.3 6.4 %copy-start.3 = (bf16[4,6,320,512]{3,2,1,0:T(8,128)(2,1)}, bf16[4,6,320,512]{3,2,1,0:T(8,128)(2,1)S(1)}, u32[]{:S(2)}) copy-start(bf16[4,6,320,512]{3,2,1,0:T(8,128)(2,1)S(1)} %broadcast_select_fusion.1) | copy-start | bytes 23592964
  43.7 5.5 %copy-start.7 = (bf16[16,320]{1,0:T(8,128)(2,1)S(1)}, bf16[16,320]{1,0:T(8,128)(2,1)}, u32[]{:S(2)}) copy-start(bf16[16,320]{1,0:T(8,128)(2,1)} %param.15) | copy-start | bytes 30724
  59.9 25.4 %copy-start.8 = (f32[1000]{0:T(1024)S(1)}, f32[1000]{0:T(1024)}, u32[]{:S(2)}) copy-start(f32[1000]{0:T(1024)} %param.17) | copy-start | bytes 12004
  66.7 73.6 %all-gather.7.cloned.1.call-start = ((), (), s32[]{:S(2)}) async-start(), calls=%async_computation.1 | async-start | bytes 1572864 | tf_op jit(solution)/shard_map/all_gather | solution.py:128
  80.3 5.5 %collective-permute-start.2 = (bf16[4,1,16,512]{3,2,1,0:T(8,128)(2,1)S(1)}, bf16[4,1,16,512]{3,2,1,0:T(8,128)(2,1)S(1)}, u32[]{:S(2)}, u32[]{:S(2)}) collective-permute-start(bf16[4,1,16,512]{3,2,1,0:T(8,128)(2,1)S(1)} %get-tuple-element.75), channel_id=1, source_target_pairs={{0,1},{1,2},{2,3},{3,4},{4,5},{5,6},{6,7},{8,9},{9,10},{10,11},{11... | collective-permute-start | bytes 196616 | tf_op jit(solution)/shard_map/ppermute | solution.py:20
  84.0 6.2 %collective-permute-start.3 = (bf16[4,1,16,512]{3,2,1,0:T(8,128)(2,1)S(1)}, bf16[4,1,16,512]{3,2,1,0:T(8,128)(2,1)S(1)}, u32[]{:S(2)}, u32[]{:S(2)}) collective-permute-start(bf16[4,1,16,512]{3,2,1,0:T(8,128)(2,1)S(1)} %get-tuple-element.76), channel_id=1, source_target_pairs={{1,0},{2,1},{3,2},{4,3},{5,4},{6,5},{7,6},{9,8},{10,9},{11,10},{12... | collective-permute-start | bytes 196616 | tf_op jit(solution)/shard_map/ppermute | solution.py:22
  93.8 0.9 copy-start.6
  100.6 6.4 %copy-start.2 = (bf16[4,6,320,512]{3,2,1,0:T(8,128)(2,1)}, bf16[4,6,320,512]{3,2,1,0:T(8,128)(2,1)S(1)}, u32[]{:S(2)}) copy-start(bf16[4,6,320,512]{3,2,1,0:T(8,128)(2,1)S(1)} %broadcast_select_fusion) | copy-start | bytes 23592964
  112.5 29.8 %copy-start.1 = (f32[1000,320]{0,1:T(8,128)S(1)}, f32[1000,320]{0,1:T(8,128)}, u32[]{:S(2)}) copy-start(f32[1000,320]{0,1:T(8,128)} %param.16) | copy-start | bytes 3840004
Sparse Core Ops, SparseCore 0:
  66.8 11.4 all-gather.4
  130.3 10.0 all-gather.6
where the time goes:
time: 150 us; the launch traced here: 149 us
  matrix products  66.5 us (44%)
  other arithmetic  22.7 us (15%)
  waiting for transfers between devices  21 us (14%)
  between operations  15.1 us (10%)
  starting transfers between devices  11.1 us (7%)
  blocking collectives  8.02 us (5%)
  local copies, waits for them, and re-layouts  4.67 us (3%)
    dot_general x4, matrix products, local(): jnp.einsum('oc,tfcp->tfop', temporal_weight[lagged], framed[:, lagged:lag...  23.3 us
    dot_general x2, matrix products, local(): jnp.einsum('ch,tfhp->tfcp', out_weight, second, preferred_element_type=jn...  21.6 us
    all_gather x2, waiting for transfers between devices, local(): lax.all_gather(updated, 'tm', axis=0, tiled=True)  16.3 us
    dot_general x2, matrix products, spatial(): jnp.einsum('oc,tfcp->tfop', spatial_weight, columns, preferred_element_ty...  11.7 us
    ppermute x2, starting transfers between devices, with_halo(): lax.ppermute(tail, axis, [(i, (i + 1) % count) for i in range(ends)])  8.51 us
    dot_general x2, matrix products, spatial(): jnp.einsum('tfcp,spq->tfscq', latent, shift_table(), preferred_element_ty...  7.45 us
    unnamed x8, other arithmetic  7.25 us
    ppermute x2, waiting for transfers between devices, with_halo(): lax.ppermute(head, axis, [((i + 1) % count, i) for i in range(ends)])  4.28 us
  transfers between devices with their start and end apart: 6, of which 4 were waited for; matrix products, arithmetic and copies ran while one was open for 9% of the time, Pallas kernels for 0%

commit v1 on v0

v1 whole, which is shorter than its diff:
```python
import functools

import jax
import jax.numpy as jnp
from jax import lax
from jax.experimental import pallas as pl
from jax.experimental.pallas import tpu as pltpu
from jax.sharding import PartitionSpec as P

HEIGHT = 16
WIDTH = 32
ITERS = 2
CHUNK = 256
MESH = pl.DeviceIdType.MESH


def kernel(
    slabs,
    ranks,
    states_ref,
    spatial_ref,
    temporal_ref,
    out_weight_ref,
    embed_ref,
    step_ref,
    index_ref,
    slides_ref,
    result_ref,
    latent,
    first,
    held,
    wide_spatial,
    wide_temporal,
    column_embed,
    edges_0,
    inner_0,
    edges_1,
    inner_1,
    halo_send,
    halo_recv,
    sum_send,
    sum_recv,
):
    times, frames, channels, cells = states_ref.shape
    window = times * ranks
    hidden = spatial_ref.shape[0]
    rank = lax.axis_index("tm")
    slab = lax.axis_index("slab")
    has_left = slab > 0
    has_right = slab < slabs - 1
    edges = (edges_0, edges_1)
    inner = (inner_0, inner_1)

    barrier = pltpu.get_barrier_semaphore()

    @pl.when(has_left)
    def _():
        pl.semaphore_signal(barrier, inc=1, device_id={"slab": slab - 1}, device_id_type=MESH)

    @pl.when(has_right)
    def _():
        pl.semaphore_signal(barrier, inc=1, device_id={"slab": slab + 1}, device_id_type=MESH)

    for ahead in range(1, ranks):
        partner = lax.rem(rank + ahead, ranks)
        pl.semaphore_signal(barrier, inc=1, device_id={"tm": partner}, device_id_type=MESH)

    cell = lax.broadcasted_iota(jnp.int32, (channels, cells), 1)
    row, col = cell // WIDTH, cell % WIDTH
    keep = lambda flag: jnp.where(flag, 1.0, 0.0).astype(jnp.float32)
    has_west, has_east = keep(col > 0), keep(col < WIDTH - 1)
    has_north, has_south = keep(row > 0), keep(row < HEIGHT - 1)

    for frame in range(frames):
        for time in range(times):
            latent[0, frame + 1, time] = states_ref[time, frame].astype(jnp.bfloat16)

    def halo_copy(sweep, side):
        source, target, place = (1, frames + 1, slab - 1) if side == 0 else (frames, 0, slab + 1)
        return pltpu.make_async_remote_copy(
            src_ref=latent.at[sweep, source],
            dst_ref=latent.at[sweep, target],
            send_sem=halo_send.at[sweep, side],
            recv_sem=halo_recv.at[sweep, side],
            device_id={"slab": place},
            device_id_type=MESH,
        )

    def start_halo(sweep):
        @pl.when(has_left)
        def _():
            halo_copy(sweep, 0).start()

        @pl.when(has_right)
        def _():
            halo_copy(sweep, 1).start()

    def wait_halo(sweep):
        @pl.when(has_left)
        def _():
            halo_copy(sweep, 0).wait_send()
            halo_copy(sweep, 1).wait_recv()

        @pl.when(has_right)
        def _():
            halo_copy(sweep, 1).wait_send()
            halo_copy(sweep, 0).wait_recv()

    zero_frame = jnp.zeros((times, channels, cells), jnp.bfloat16)
    for sweep in range(ITERS):

        @pl.when(jnp.logical_not(has_left))
        def _():
            latent[sweep, 0] = zero_frame

        @pl.when(jnp.logical_not(has_right))
        def _():
            latent[sweep, frames + 1] = zero_frame

    greeted = has_left.astype(jnp.int32) + has_right.astype(jnp.int32) + (ranks - 1)
    pl.semaphore_wait(barrier, greeted)
    start_halo(0)

    half = jnp.asarray(0.5, jnp.bfloat16)
    wide_spatial[...] = spatial_ref[...] * half
    for lag in range(3):
        wide_temporal[:, lag * hidden : (lag + 1) * hidden] = temporal_ref[lag] * half

    def silu_half(h):
        return h + h * jnp.tanh(h)

    def first_of(sweep, place, valid):
        for time in range(times):
            x = latent[sweep, place, time].astype(jnp.float32)
            west = pltpu.roll(x, 1, 1) * has_west
            east = pltpu.roll(x, cells - 1, 1) * has_east
            mids = (west, x, east)
            above = [pltpu.roll(m, WIDTH, 1) * has_north for m in mids]
            below = [pltpu.roll(m, cells - WIDTH, 1) * has_south for m in mids]
            columns = jnp.concatenate(above + list(mids) + below, axis=0).astype(jnp.bfloat16)
            for at in range(0, cells, CHUNK):
                h = jnp.dot(
                    wide_spatial[...],
                    columns[:, at : at + CHUNK],
                    preferred_element_type=jnp.float32,
                )
                shift = column_embed[time]
                h = h + jnp.concatenate([shift] * (CHUNK // 128), axis=1)
                value = silu_half(h)
                if valid is not None:
                    value = value * valid
                first[time, place, :, at : at + CHUNK] = value.astype(jnp.bfloat16)

    def sums_of(steps, anchors, sums, frame, slot):
        for at in range(0, cells, CHUNK):
            lanes = slice(at, at + CHUNK)
            total = anchors(frame, lanes)
            for time in range(times):
                framed = first[time, pl.ds(frame, 3), :, lanes].reshape(3 * hidden, CHUNK)
                h = jnp.dot(wide_temporal[...], framed, preferred_element_type=jnp.float32)
                second = silu_half(h).astype(jnp.bfloat16)
                drift = jnp.dot(out_weight_ref[...], second, preferred_element_type=jnp.float32)
                total = total + steps[time] * drift
                sums[slot, rank * times + time, :, lanes] = total

    def sum_copy(sweep, sums, slot, frame, ahead, place):
        block = sums.at[slot, pl.ds(place * times, times)]
        return pltpu.make_async_remote_copy(
            src_ref=block,
            dst_ref=block,
            send_sem=sum_send.at[sweep, frame, ahead - 1],
            recv_sem=sum_recv.at[sweep, frame, ahead - 1],
            device_id={"tm": lax.rem(rank + ahead, ranks)},
            device_id_type=MESH,
        )

    def start_sums(sweep, sums, slot, frame):
        for ahead in range(1, ranks):
            sum_copy(sweep, sums, slot, frame, ahead, rank).start()

    def wait_sums(sweep, sums, slot, frame):
        for ahead in range(1, ranks):
            sum_copy(sweep, sums, slot, frame, ahead, rank).wait_send()
            source = lax.rem(rank + ranks - ahead, ranks)
            sum_copy(sweep, sums, slot, frame, ahead, source).wait_recv()

    def moved(sweep, sums, slot, time):
        place = slides_ref[sweep] + rank * times + time - 1
        place = jnp.clip(place, 0, window - 1)
        value = sums[slot, place]
        for lower in range(1, ranks):
            weight = jnp.where(place >= lower * times, 1.0, 0.0).astype(jnp.float32)
            value = value + weight * sums[slot, lower * times - 1]
        return value

    def new_states(sweep, sums, slot, frame):
        for time in range(times):
            value = moved(sweep, sums, slot, time)
            if sweep == ITERS - 1:
                result_ref[time, frame] = value
            else:
                if time == 0:
                    held[frame] = value
                latent[sweep + 1, frame + 1, time] = value.astype(jnp.bfloat16)

    edge_frames = (0, frames - 1)
    inner_frames = tuple(range(1, frames - 1))
    lead = jnp.where(rank == 0, 1.0, 0.0).astype(jnp.float32)
    offset = jnp.int32(0)
    for sweep in range(ITERS):
        steps = []
        for time in range(times):
            place = index_ref[offset + rank * times + time]
            steps.append(step_ref[place])
            line = embed_ref[pl.ds(place, 1), :] * 0.5
            column_embed[time] = jnp.transpose(jnp.broadcast_to(line, (128, hidden)))
        offset = offset + slides_ref[sweep]

        if sweep == 0:
            anchors = lambda frame, lanes: states_ref[0, frame, :, lanes] * lead
        else:
            anchors = lambda frame, lanes: held[frame, :, lanes] * lead

        @pl.loop(0, 2)
        def _(side):
            first_of(sweep, 1 + side * (frames - 1), None)

        if sweep > 0:
            for slot, frame in enumerate(inner_frames):
                wait_sums(sweep - 1, inner[sweep - 1], slot, frame)
            for slot, frame in enumerate(inner_frames):
                new_states(sweep - 1, inner[sweep - 1], slot, frame)

        @pl.loop(2, frames)
        def _(place):
            first_of(sweep, place, None)

        def edge_sums():
            wait_halo(sweep)

            @pl.loop(0, 2)
            def _(side):
                exists = jnp.where(side == 0, slab > 0, slab < slabs - 1)
                valid = jnp.where(exists, 1.0, 0.0).astype(jnp.float32)
                first_of(sweep, side * (frames + 1), valid)

            @pl.loop(0, 2)
            def _(side):
                frame = side * (frames - 1)
                sums_of(steps, anchors, edges[sweep], frame, side)
                start_sums(sweep, edges[sweep], side, frame)

        def inner_sums():
            @pl.loop(1, frames - 1)
            def _(frame):
                sums_of(steps, anchors, inner[sweep], frame, frame - 1)
                start_sums(sweep, inner[sweep], frame - 1, frame)

        def edge_states():
            for slot, frame in enumerate(edge_frames):
                wait_sums(sweep, edges[sweep], slot, frame)
            for slot, frame in enumerate(edge_frames):
                new_states(sweep, edges[sweep], slot, frame)

        if sweep < ITERS - 1:
            edge_sums()
            inner_sums()
            edge_states()
            start_halo(sweep + 1)
        else:
            inner_sums()
            edge_sums()
            for slot, frame in enumerate(inner_frames):
                wait_sums(sweep, inner[sweep], slot, frame)
            for slot, frame in enumerate(inner_frames):
                new_states(sweep, inner[sweep], slot, frame)
            edge_states()


def local(slabs, ranks, window_states, spatial_weight, temporal_weight, out_weight, time_embed, step_size, time_index, slides):
    times, frames, channels, cells = window_states.shape
    hidden = spatial_weight.shape[0]
    window = times * ranks
    f32, bf16 = jnp.float32, jnp.bfloat16
    vmem = pl.BlockSpec(memory_space=pltpu.VMEM)
    smem = pl.BlockSpec(memory_space=pltpu.SMEM)
    return pl.pallas_call(
        functools.partial(kernel, slabs, ranks),
        out_shape=jax.ShapeDtypeStruct(window_states.shape, f32),
        in_specs=[vmem] * 5 + [smem] * 3,
        out_specs=vmem,
        scratch_shapes=[
            pltpu.VMEM((ITERS, frames + 2, times, channels, cells), bf16),
            pltpu.VMEM((times, frames + 2, hidden, cells), bf16),
            pltpu.VMEM((frames, channels, cells), f32),
            pltpu.VMEM(spatial_weight.shape, bf16),
            pltpu.VMEM((hidden, 3 * hidden), bf16),
            pltpu.VMEM((times, hidden, 128), f32),
            pltpu.VMEM((2, window, channels, cells), f32),
            pltpu.VMEM((frames - 2, window, channels, cells), f32),
            pltpu.VMEM((2, window, channels, cells), f32),
            pltpu.VMEM((frames - 2, window, channels, cells), f32),
            pltpu.SemaphoreType.DMA((ITERS, 2)),
            pltpu.SemaphoreType.DMA((ITERS, 2)),
            pltpu.SemaphoreType.DMA((ITERS, frames, ranks - 1)),
            pltpu.SemaphoreType.DMA((ITERS, frames, ranks - 1)),
        ],
        compiler_params=pltpu.CompilerParams(
            collective_id=0, has_side_effects=True, vmem_limit_bytes=48 * 1024 * 1024
        ),
    )(window_states, spatial_weight, temporal_weight, out_weight, time_embed, step_size, time_index, slides)


def solution(mesh):
    return jax.shard_map(
        functools.partial(local, mesh.shape["slab"], mesh.shape["tm"]),
        mesh=mesh,
        in_specs=(
            P("tm", ("groups", "slab"), None, None),
            P(),
            P(),
            P(),
            P(),
            P(),
            P("groups"),
            P("groups"),
        ),
        out_specs=P("tm", ("groups", "slab"), None, None),
        check_vma=False,
    )
```

time: 150 us -> 52.7 us (0.35)
  matrix products: 66.5 us -> 0 us
  Pallas kernels: 0 us -> 48.8 us
  other arithmetic: 22.7 us -> 0 us
  waiting for transfers between devices: 21 us -> 0 us
  between operations: 15.1 us -> 0.09 us
  starting transfers between devices: 11.1 us -> 0 us
  blocking collectives: 8.02 us -> 0 us
    dot_general x14 -> x0, matrix products: 66.5 us -> none  [the longest x4 23.3 us: local(): jnp.einsum('oc,tfcp->tfop', temporal_weight[lagged], framed[:, lagged:lag...]
    pallas_call x0 -> x1, Pallas kernels: none -> 48.8 us  [local(): pl.pallas_call(functools.partial(kernel, slabs, ranks), out_shape=jax.Sha...]
    all_gather x2 -> x0, waiting for transfers between devices: 16.3 us -> none  [local(): lax.all_gather(updated, 'tm', axis=0, tiled=True)]
    ppermute x4 -> x0, starting transfers between devices: 11.1 us -> none  [the longest x2 8.51 us: with_halo(): lax.ppermute(tail, axis, [(i, (i + 1) % count) for i in range(ends)])]
    all_gather x4 -> x0, blocking collectives: 8.02 us -> none  [the longest x2 4.03 us: local(): lax.all_gather(ending[None], 'tm', axis=0, tiled=True)]
    unnamed x8 -> x0, other arithmetic: 7.25 us -> none
    add x15 -> x0, other arithmetic: 5.61 us -> none  [the longest x2 1.87 us: local(): ending = anchor + summed]
    another operation x3 -> x0, other arithmetic: 4.81 us -> none  [the longest x2 3.94 us: local(): running = jnp.cumsum(weighted, axis=0)]
  transfers between devices with their start and end apart: 6 -> 0, of which waited for: 4 -> 0; matrix products, arithmetic and copies ran while one was open for 9% -> 0% of each run, Pallas kernels for 0% -> 0%
where the time goes in v1:
time: 52.7 us; the launch traced here: 52.6 us
  Pallas kernels  48.8 us (93%)
  local copies, waits for them, and re-layouts  3.71 us (7%)
    pallas_call x1, Pallas kernels, local(): pl.pallas_call(functools.partial(kernel, slabs, ranks), out_shape=jax.Sha...  48.8 us
    unnamed x15, local copies, waits for them, and re-layouts  3.71 us

profile of v1, /device:TPU:0, one launch (start us, length us, event | category | flops | bytes accessed | tf_op | source)
XLA Modules:
  0.0 52.6 jit_solution(14817128342569477879)
XLA Ops:
  0.0 0.0 copy-start.5
  0.0 0.0 copy-start.4
  0.0 0.0 copy-start.3
  0.0 0.0 copy-start.2
  0.0 0.0 copy-start
  0.0 0.0 copy-start.1
  0.0 1.1 %copy.9.spatial_ref = bf16[320,144]{1,0:T(8,128)(2,1)S(1)} copy(bf16[320,144]{0,1:T(8,128)(2,1)} %param.9) | data formatting | bytes 184320 | tf_op args[1]
  1.1 1.8 %copy.10.embed_ref = f32[1000,320]{1,0:T(8,128)S(1)} copy(f32[1000,320]{0,1:T(8,128)} %param.12) | data formatting | bytes 2560000 | tf_op args[4]
  2.9 0.0 copy-done.5
  2.9 0.0 copy-done.4
  2.9 0.0 copy-done.3
  3.0 0.0 copy-done.2
  3.0 0.0 copy-done
  3.0 0.0 copy-done.1
  3.0 48.8 %shard_map.82 = f32[4,4,16,512]{3,2,1,0:T(8,128)S(1)} custom-call(f32[4,4,16,512]{3,2,1,0:T(8,128)S(1)} %copy-done.1, bf16[320,144]{1,0:T(8,128)(2,1)S(1)} %copy.9.spatial_ref, bf16[3,320,320]{2,1,0:T(8,128)(2,1)S(1)} %copy-done, bf16[16,320]{1,0:T(8,128)(2,1)S(1)} %copy-done.2, f32[1000,320]{1,0:T(8,128)S(1)} %copy.10.embed_ref, f32[1000]{0:T(1024)S(1)} %copy-done.3, ...), custom_call_target="tpu_custom_call" | custom-call | tf_op jit(solution)/shard_map/pallas_call | solution.py:287
  51.8 0.8 %copy.12 = f32[4,4,16,512]{3,2,1,0:T(8,128)} copy(f32[4,4,16,512]{3,2,1,0:T(8,128)S(1)} %shard_map.82) | data formatting | bytes 1048576
Async XLA Ops:
  0.0 2.9 %copy-start.5 = (s32[2]{0:T(128)S(1)}, s32[2]{0:T(128)}, u32[]{:S(2)}) copy-start(s32[2]{0:T(128)} %slides_ref.1) | copy-start | bytes 28
  0.0 2.9 %copy-start.4 = (s32[24]{0:T(128)S(1)}, s32[24]{0:T(128)}, u32[]{:S(2)}) copy-start(s32[24]{0:T(128)} %index_ref.1) | copy-start | bytes 292
  0.0 2.9 %copy-start.3 = (f32[1000]{0:T(1024)S(1)}, f32[1000]{0:T(1024)}, u32[]{:S(2)}) copy-start(f32[1000]{0:T(1024)} %step_ref.1) | copy-start | bytes 12004
  0.0 3.0 %copy-start.2 = (bf16[16,320]{1,0:T(8,128)(2,1)S(1)}, bf16[16,320]{1,0:T(8,128)(2,1)}, u32[]{:S(2)}) copy-start(bf16[16,320]{1,0:T(8,128)(2,1)} %out_weight_ref.1) | copy-start | bytes 30724
  0.0 3.0 %copy-start = (bf16[3,320,320]{2,1,0:T(8,128)(2,1)S(1)}, bf16[3,320,320]{2,1,0:T(8,128)(2,1)}, u32[]{:S(2)}) copy-start(bf16[3,320,320]{2,1,0:T(8,128)(2,1)} %temporal_ref.1) | copy-start | bytes 1843204
  0.0 3.0 %copy-start.1 = (f32[4,4,16,512]{3,2,1,0:T(8,128)S(1)}, f32[4,4,16,512]{3,2,1,0:T(8,128)}, u32[]{:S(2)}) copy-start(f32[4,4,16,512]{3,2,1,0:T(8,128)} %states_ref.1) | copy-start | bytes 1572868

commit v2 on v1

--- a/solution.py
+++ b/solution.py
@@ -10,7 +10,7 @@
 HEIGHT = 16
 WIDTH = 32
 ITERS = 2
-CHUNK = 256
+CHUNK = 512
 MESH = pl.DeviceIdType.MESH
 
 
@@ -43,7 +43,7 @@
 ):
     times, frames, channels, cells = states_ref.shape
     window = times * ranks
-    hidden = spatial_ref.shape[0]
+    hidden = spatial_ref.shape[1]
     rank = lax.axis_index("tm")
     slab = lax.axis_index("slab")
     has_left = slab > 0
@@ -122,9 +122,25 @@
     start_halo(0)
 
     half = jnp.asarray(0.5, jnp.bfloat16)
-    wide_spatial[...] = spatial_ref[...] * half
+    turned = jnp.transpose(spatial_ref[...].astype(jnp.float32))
+    wide_spatial[...] = (turned * 0.5).astype(jnp.bfloat16)
     for lag in range(3):
         wide_temporal[:, lag * hidden : (lag + 1) * hidden] = temporal_ref[lag] * half
+
+    def embed_column(place):
+        steps = embed_ref.shape[1]
+        lane = lax.broadcasted_iota(jnp.int32, (hidden, 128), 1)
+        picked = jnp.zeros((hidden, 128), jnp.float32)
+        full = steps // 128 * 128
+        for at in range(0, full, 128):
+            picked = jnp.where(lane == place - at, embed_ref[:, at : at + 128], picked)
+        column = jnp.sum(picked, axis=1, keepdims=True)
+        if steps > full:
+            block = embed_ref[:, full:]
+            lane = lax.broadcasted_iota(jnp.int32, block.shape, 1)
+            picked = jnp.where(lane == place - full, block, 0.0)
+            column = column + jnp.sum(picked, axis=1, keepdims=True)
+        return column
 
     def silu_half(h):
         return h + h * jnp.tanh(h)
@@ -212,8 +228,8 @@
         for time in range(times):
             place = index_ref[offset + rank * times + time]
             steps.append(step_ref[place])
-            line = embed_ref[pl.ds(place, 1), :] * 0.5
-            column_embed[time] = jnp.transpose(jnp.broadcast_to(line, (128, hidden)))
+            column = embed_column(place) * 0.5
+            column_embed[time] = jnp.broadcast_to(column, (hidden, 128))
         offset = offset + slides_ref[sweep]
 
         if sweep == 0:
@@ -308,7 +324,7 @@
         compiler_params=pltpu.CompilerParams(
             collective_id=0, has_side_effects=True, vmem_limit_bytes=48 * 1024 * 1024
         ),
-    )(window_states, spatial_weight, temporal_weight, out_weight, time_embed, step_size, time_index, slides)
+    )(window_states, spatial_weight.T, temporal_weight, out_weight, time_embed.T, step_size, time_index, slides)
 
 
 def solution(mesh):

time: 52.7 us -> 42.2 us (0.80)
  Pallas kernels: 48.8 us -> 33.9 us
  local copies, waits for them, and re-layouts: 3.71 us -> 7.87 us
    pallas_call x1, Pallas kernels: 48.8 us -> 33.9 us  [local(): pl.pallas_call(functools.partial(kernel, slabs, ranks), out_shape=jax.Sha...]
    unnamed x15 -> x17, local copies, waits for them, and re-layouts: 3.71 us -> 7.87 us
where the time goes in v2:
time: 42.2 us; the launch traced here: 41.8 us
  Pallas kernels  33.9 us (80%)
  local copies, waits for them, and re-layouts  7.87 us (19%)
    pallas_call x1, Pallas kernels, local(): pl.pallas_call(functools.partial(kernel, slabs, ranks), out_shape=jax.Sha...  33.9 us
    unnamed x17, local copies, waits for them, and re-layouts  7.87 us

profile of v2, /device:TPU:0, one launch (start us, length us, event | category | flops | bytes accessed | tf_op | source)
XLA Modules:
  0.0 41.8 jit_solution(14775812858146233282)
XLA Ops:
  0.0 0.0 copy-start
  0.0 1.3 %copy-done = f32[1000,320]{0,1:T(8,128)S(1)} copy-done((f32[1000,320]{0,1:T(8,128)S(1)}, f32[1000,320]{0,1:T(8,128)}, u32[]{:S(2)}) %copy-start) | copy-done | bytes 1280024
  1.3 0.0 copy-start.1
  1.3 1.1 %copy-done.1 = bf16[3,320,320]{2,1,0:T(8,128)(2,1)S(1)} copy-done((bf16[3,320,320]{2,1,0:T(8,128)(2,1)S(1)}, bf16[3,320,320]{2,1,0:T(8,128)(2,1)}, u32[]{:S(2)}) %copy-start.1) | copy-done | bytes 614424
  2.4 0.0 copy-start.2
  2.4 1.0 %copy-done.2 = f32[4,4,16,512]{3,2,1,0:T(8,128)S(1)} copy-done((f32[4,4,16,512]{3,2,1,0:T(8,128)S(1)}, f32[4,4,16,512]{3,2,1,0:T(8,128)}, u32[]{:S(2)}) %copy-start.2) | copy-done | bytes 524312
  3.5 0.0 copy-start.3
  3.5 0.9 %copy-done.3 = bf16[320,144]{0,1:T(8,128)(2,1)S(1)} copy-done((bf16[320,144]{0,1:T(8,128)(2,1)S(1)}, bf16[320,144]{0,1:T(8,128)(2,1)}, u32[]{:S(2)}) %copy-start.3) | copy-done | bytes 92184
  4.4 0.0 copy-start.4
  4.4 0.7 %copy-done.4 = bf16[16,320]{1,0:T(8,128)(2,1)S(1)} copy-done((bf16[16,320]{1,0:T(8,128)(2,1)S(1)}, bf16[16,320]{1,0:T(8,128)(2,1)}, u32[]{:S(2)}) %copy-start.4) | copy-done | bytes 10264
  5.1 0.0 copy-start.5
  5.1 0.7 %copy-done.5 = f32[1000]{0:T(1024)S(1)} copy-done((f32[1000]{0:T(1024)S(1)}, f32[1000]{0:T(1024)}, u32[]{:S(2)}) %copy-start.5) | copy-done | bytes 4024
  5.8 0.0 copy-start.6
  5.8 0.7 %copy-done.6 = s32[24]{0:T(128)S(1)} copy-done((s32[24]{0:T(128)S(1)}, s32[24]{0:T(128)}, u32[]{:S(2)}) %copy-start.6) | copy-done | bytes 120
  6.4 0.0 copy-start.7
  6.4 0.7 %copy-done.7 = s32[2]{0:T(128)S(1)} copy-done((s32[2]{0:T(128)S(1)}, s32[2]{0:T(128)}, u32[]{:S(2)}) %copy-start.7) | copy-done | bytes 32
  7.1 33.9 %shard_map.82 = f32[4,4,16,512]{3,2,1,0:T(8,128)S(1)} custom-call(f32[4,4,16,512]{3,2,1,0:T(8,128)S(1)} %copy-done.2, bf16[144,320]{1,0:T(8,128)(2,1)S(1)} %bitcast.3, bf16[3,320,320]{2,1,0:T(8,128)(2,1)S(1)} %copy-done.1, bf16[16,320]{1,0:T(8,128)(2,1)S(1)} %copy-done.4, f32[320,1000]{1,0:T(8,128)S(1)} %bitcast.2, f32[1000]{0:T(1024)S(1)} %copy-done.5, ...), custom_call_target="tpu_custom_call" | custom-call | tf_op jit(solution)/shard_map/pallas_call | solution.py:303
  41.0 0.8 %copy.10 = f32[4,4,16,512]{3,2,1,0:T(8,128)} copy(f32[4,4,16,512]{3,2,1,0:T(8,128)S(1)} %shard_map.82) | data formatting | bytes 1048576
Async XLA Ops:
  0.0 1.3 %copy-start = (f32[1000,320]{0,1:T(8,128)S(1)}, f32[1000,320]{0,1:T(8,128)}, u32[]{:S(2)}) copy-start(f32[1000,320]{0,1:T(8,128)} %param.12) | copy-start | bytes 3840004
  1.3 1.1 %copy-start.1 = (bf16[3,320,320]{2,1,0:T(8,128)(2,1)S(1)}, bf16[3,320,320]{2,1,0:T(8,128)(2,1)}, u32[]{:S(2)}) copy-start(bf16[3,320,320]{2,1,0:T(8,128)(2,1)} %temporal_ref.1) | copy-start | bytes 1843204
  2.4 1.0 %copy-start.2 = (f32[4,4,16,512]{3,2,1,0:T(8,128)S(1)}, f32[4,4,16,512]{3,2,1,0:T(8,128)}, u32[]{:S(2)}) copy-start(f32[4,4,16,512]{3,2,1,0:T(8,128)} %states_ref.1) | copy-start | bytes 1572868
  3.5 0.9 %copy-start.3 = (bf16[320,144]{0,1:T(8,128)(2,1)S(1)}, bf16[320,144]{0,1:T(8,128)(2,1)}, u32[]{:S(2)}) copy-start(bf16[320,144]{0,1:T(8,128)(2,1)} %param.9) | copy-start | bytes 276484
  4.4 0.7 %copy-start.4 = (bf16[16,320]{1,0:T(8,128)(2,1)S(1)}, bf16[16,320]{1,0:T(8,128)(2,1)}, u32[]{:S(2)}) copy-start(bf16[16,320]{1,0:T(8,128)(2,1)} %out_weight_ref.1) | copy-start | bytes 30724
  5.1 0.7 %copy-start.5 = (f32[1000]{0:T(1024)S(1)}, f32[1000]{0:T(1024)}, u32[]{:S(2)}) copy-start(f32[1000]{0:T(1024)} %step_ref.1) | copy-start | bytes 12004
  5.8 0.7 %copy-start.6 = (s32[24]{0:T(128)S(1)}, s32[24]{0:T(128)}, u32[]{:S(2)}) copy-start(s32[24]{0:T(128)} %index_ref.1) | copy-start | bytes 292
  6.4 0.7 %copy-start.7 = (s32[2]{0:T(128)S(1)}, s32[2]{0:T(128)}, u32[]{:S(2)}) copy-start(s32[2]{0:T(128)} %slides_ref.1) | copy-start | bytes 28

commit v3 on v2

--- a/solution.py
+++ b/solution.py
@@ -10,7 +10,7 @@
 HEIGHT = 16
 WIDTH = 32
 ITERS = 2
-CHUNK = 512
+UNIT = 256
 MESH = pl.DeviceIdType.MESH
 
 
@@ -31,6 +31,7 @@
     held,
     wide_spatial,
     wide_temporal,
+    wide_out,
     column_embed,
     edges_0,
     inner_0,
@@ -127,6 +128,13 @@
     for lag in range(3):
         wide_temporal[:, lag * hidden : (lag + 1) * hidden] = temporal_ref[lag] * half
 
+    minor = hidden % UNIT
+    major = hidden - minor
+    wide_out[...] = jnp.zeros_like(wide_out)
+    for time in range(times):
+        rows, lanes = slice(time * channels, (time + 1) * channels), slice(time * minor, (time + 1) * minor)
+        wide_out[rows, lanes] = out_weight_ref[:, major:]
+
     def embed_column(place):
         steps = embed_ref.shape[1]
         lane = lax.broadcasted_iota(jnp.int32, (hidden, 128), 1)
@@ -145,39 +153,67 @@
     def silu_half(h):
         return h + h * jnp.tanh(h)
 
-    def first_of(sweep, place, valid):
-        for time in range(times):
-            x = latent[sweep, place, time].astype(jnp.float32)
-            west = pltpu.roll(x, 1, 1) * has_west
-            east = pltpu.roll(x, cells - 1, 1) * has_east
-            mids = (west, x, east)
-            above = [pltpu.roll(m, WIDTH, 1) * has_north for m in mids]
-            below = [pltpu.roll(m, cells - WIDTH, 1) * has_south for m in mids]
-            columns = jnp.concatenate(above + list(mids) + below, axis=0).astype(jnp.bfloat16)
-            for at in range(0, cells, CHUNK):
+    def columns_of(sweep, place, time):
+        x = latent[sweep, place, time].astype(jnp.float32)
+        west = pltpu.roll(x, 1, 1) * has_west
+        east = pltpu.roll(x, cells - 1, 1) * has_east
+        mids = (west, x, east)
+        above = [pltpu.roll(m, WIDTH, 1) * has_north for m in mids]
+        below = [pltpu.roll(m, cells - WIDTH, 1) * has_south for m in mids]
+        return jnp.concatenate(above + list(mids) + below, axis=0).astype(jnp.bfloat16)
+
+    def first_of(sweep, places):
+        def finish(place, time, valid, h):
+            shift = column_embed[time]
+            value = silu_half(h + jnp.concatenate([shift] * (cells // 128), axis=1))
+            if valid is not None:
+                value = value * valid
+            first[time, place] = value.astype(jnp.bfloat16)
+
+        behind = None
+        for place, valid in places:
+            for time in range(times):
                 h = jnp.dot(
                     wide_spatial[...],
-                    columns[:, at : at + CHUNK],
+                    columns_of(sweep, place, time),
                     preferred_element_type=jnp.float32,
                 )
-                shift = column_embed[time]
-                h = h + jnp.concatenate([shift] * (CHUNK // 128), axis=1)
-                value = silu_half(h)
-                if valid is not None:
-                    value = value * valid
-                first[time, place, :, at : at + CHUNK] = value.astype(jnp.bfloat16)
-
-    def sums_of(steps, anchors, sums, frame, slot):
-        for at in range(0, cells, CHUNK):
-            lanes = slice(at, at + CHUNK)
-            total = anchors(frame, lanes)
+                if behind is not None:
+                    finish(*behind)
+                behind = (place, time, valid, h)
+        finish(*behind)
+
+    def sums_of(steps, anchors, sums, places, done):
+        def project(frame, slot, seconds):
+            rests = jnp.concatenate([second[major:] for second in seconds], axis=0)
+            rest = jnp.dot(wide_out[...], rests, preferred_element_type=jnp.float32)
+            total = anchors(frame)
+            for time, second in enumerate(seconds):
+                drift = jnp.dot(
+                    out_weight_ref[:, :major], second[:major], preferred_element_type=jnp.float32
+                )
+                drift = drift + rest[time * channels : (time + 1) * channels]
+                total = total + steps[time] * drift
+                sums[slot, rank * times + time] = total
+            done(slot, frame)
+
+        behind = None
+        seconds = []
+
+        def finish(frame, slot, h):
+            seconds.append(silu_half(h).astype(jnp.bfloat16))
+            if len(seconds) == times:
+                project(frame, slot, list(seconds))
+                seconds.clear()
+
+        for slot, frame in enumerate(places):
             for time in range(times):
-                framed = first[time, pl.ds(frame, 3), :, lanes].reshape(3 * hidden, CHUNK)
+                framed = first[time, frame : frame + 3].reshape(3 * hidden, cells)
                 h = jnp.dot(wide_temporal[...], framed, preferred_element_type=jnp.float32)
-                second = silu_half(h).astype(jnp.bfloat16)
-                drift = jnp.dot(out_weight_ref[...], second, preferred_element_type=jnp.float32)
-                total = total + steps[time] * drift
-                sums[slot, rank * times + time, :, lanes] = total
+                if behind is not None:
+                    finish(*behind)
+                behind = (frame, slot, h)
+        finish(*behind)
 
     def sum_copy(sweep, sums, slot, frame, ahead, place):
         block = sums.at[slot, pl.ds(place * times, times)]
@@ -233,13 +269,11 @@
         offset = offset + slides_ref[sweep]
 
         if sweep == 0:
-            anchors = lambda frame, lanes: states_ref[0, frame, :, lanes] * lead
+            anchors = lambda frame: states_ref[0, frame] * lead
         else:
-            anchors = lambda frame, lanes: held[frame, :, lanes] * lead
-
-        @pl.loop(0, 2)
-        def _(side):
-            first_of(sweep, 1 + side * (frames - 1), None)
+            anchors = lambda frame: held[frame] * lead
+
+        first_of(sweep, [(1, None), (frames, None)])
 
         if sweep > 0:
             for slot, frame in enumerate(inner_frames):
@@ -247,30 +281,18 @@
             for slot, frame in enumerate(inner_frames):
                 new_states(sweep - 1, inner[sweep - 1], slot, frame)
 
-        @pl.loop(2, frames)
-        def _(place):
-            first_of(sweep, place, None)
+        first_of(sweep, [(frame + 1, None) for frame in inner_frames])
 
         def edge_sums():
             wait_halo(sweep)
 
-            @pl.loop(0, 2)
-            def _(side):
-                exists = jnp.where(side == 0, slab > 0, slab < slabs - 1)
-                valid = jnp.where(exists, 1.0, 0.0).astype(jnp.float32)
-                first_of(sweep, side * (frames + 1), valid)
-
-            @pl.loop(0, 2)
-            def _(side):
-                frame = side * (frames - 1)
-                sums_of(steps, anchors, edges[sweep], frame, side)
-                start_sums(sweep, edges[sweep], side, frame)
+            first_of(sweep, [(0, keep(has_left)), (frames + 1, keep(has_right))])
+            done = lambda slot, frame: start_sums(sweep, edges[sweep], slot, frame)
+            sums_of(steps, anchors, edges[sweep], edge_frames, done)
 
         def inner_sums():
-            @pl.loop(1, frames - 1)
-            def _(frame):
-                sums_of(steps, anchors, inner[sweep], frame, frame - 1)
-                start_sums(sweep, inner[sweep], frame - 1, frame)
+            done = lambda slot, frame: start_sums(sweep, inner[sweep], slot, frame)
+            sums_of(steps, anchors, inner[sweep], inner_frames, done)
 
         def edge_states():
             for slot, frame in enumerate(edge_frames):
@@ -311,6 +333,7 @@
             pltpu.VMEM((frames, channels, cells), f32),
             pltpu.VMEM(spatial_weight.shape, bf16),
             pltpu.VMEM((hidden, 3 * hidden), bf16),
+            pltpu.VMEM((times * channels, times * (hidden % UNIT)), bf16),
             pltpu.VMEM((times, hidden, 128), f32),
             pltpu.VMEM((2, window, channels, cells), f32),
             pltpu.VMEM((frames - 2, window, channels, cells), f32),

time: 42.2 us -> 37.7 us (0.89)
  Pallas kernels: 33.9 us -> 29.4 us
    pallas_call x1, Pallas kernels: 33.9 us -> 29.4 us  [local(): pl.pallas_call(functools.partial(kernel, slabs, ranks), out_shape=jax.Sha...]
where the time goes in v3:
time: 37.7 us; the launch traced here: 37.3 us
  Pallas kernels  29.4 us (78%)
  local copies, waits for them, and re-layouts  7.87 us (21%)
    pallas_call x1, Pallas kernels, local(): pl.pallas_call(functools.partial(kernel, slabs, ranks), out_shape=jax.Sha...  29.4 us
    unnamed x17, local copies, waits for them, and re-layouts  7.87 us

profile of v3, /device:TPU:0, one launch (start us, length us, event | category | flops | bytes accessed | tf_op | source)
XLA Modules:
  0.0 37.3 jit_solution(8277434211859510131)
XLA Ops:
  0.0 0.0 copy-start
  0.0 1.3 %copy-done = f32[1000,320]{0,1:T(8,128)S(1)} copy-done((f32[1000,320]{0,1:T(8,128)S(1)}, f32[1000,320]{0,1:T(8,128)}, u32[]{:S(2)}) %copy-start) | copy-done | bytes 1280024
  1.3 0.0 copy-start.1
  1.3 1.1 %copy-done.1 = bf16[3,320,320]{2,1,0:T(8,128)(2,1)S(1)} copy-done((bf16[3,320,320]{2,1,0:T(8,128)(2,1)S(1)}, bf16[3,320,320]{2,1,0:T(8,128)(2,1)}, u32[]{:S(2)}) %copy-start.1) | copy-done | bytes 614424
  2.4 0.0 copy-start.2
  2.4 1.0 %copy-done.2 = f32[4,4,16,512]{3,2,1,0:T(8,128)S(1)} copy-done((f32[4,4,16,512]{3,2,1,0:T(8,128)S(1)}, f32[4,4,16,512]{3,2,1,0:T(8,128)}, u32[]{:S(2)}) %copy-start.2) | copy-done | bytes 524312
  3.5 0.0 copy-start.3
  3.5 0.9 %copy-done.3 = bf16[320,144]{0,1:T(8,128)(2,1)S(1)} copy-done((bf16[320,144]{0,1:T(8,128)(2,1)S(1)}, bf16[320,144]{0,1:T(8,128)(2,1)}, u32[]{:S(2)}) %copy-start.3) | copy-done | bytes 92184
  4.4 0.0 copy-start.4
  4.4 0.7 %copy-done.4 = bf16[16,320]{1,0:T(8,128)(2,1)S(1)} copy-done((bf16[16,320]{1,0:T(8,128)(2,1)S(1)}, bf16[16,320]{1,0:T(8,128)(2,1)}, u32[]{:S(2)}) %copy-start.4) | copy-done | bytes 10264
  5.1 0.0 copy-start.5
  5.1 0.7 %copy-done.5 = f32[1000]{0:T(1024)S(1)} copy-done((f32[1000]{0:T(1024)S(1)}, f32[1000]{0:T(1024)}, u32[]{:S(2)}) %copy-start.5) | copy-done | bytes 4024
  5.8 0.0 copy-start.6
  5.8 0.7 %copy-done.6 = s32[24]{0:T(128)S(1)} copy-done((s32[24]{0:T(128)S(1)}, s32[24]{0:T(128)}, u32[]{:S(2)}) %copy-start.6) | copy-done | bytes 120
  6.4 0.0 copy-start.7
  6.4 0.7 %copy-done.7 = s32[2]{0:T(128)S(1)} copy-done((s32[2]{0:T(128)S(1)}, s32[2]{0:T(128)}, u32[]{:S(2)}) %copy-start.7) | copy-done | bytes 32
  7.1 29.4 %shard_map.82 = f32[4,4,16,512]{3,2,1,0:T(8,128)S(1)} custom-call(f32[4,4,16,512]{3,2,1,0:T(8,128)S(1)} %copy-done.2, bf16[144,320]{1,0:T(8,128)(2,1)S(1)} %bitcast.3, bf16[3,320,320]{2,1,0:T(8,128)(2,1)S(1)} %copy-done.1, bf16[16,320]{1,0:T(8,128)(2,1)S(1)} %copy-done.4, f32[320,1000]{1,0:T(8,128)S(1)} %bitcast.2, f32[1000]{0:T(1024)S(1)} %copy-done.5, ...), custom_call_target="tpu_custom_call" | custom-call | tf_op jit(solution)/shard_map/pallas_call | solution.py:325
  36.5 0.8 %copy.10 = f32[4,4,16,512]{3,2,1,0:T(8,128)} copy(f32[4,4,16,512]{3,2,1,0:T(8,128)S(1)} %shard_map.82) | data formatting | bytes 1048576
Async XLA Ops:
  0.0 1.3 %copy-start = (f32[1000,320]{0,1:T(8,128)S(1)}, f32[1000,320]{0,1:T(8,128)}, u32[]{:S(2)}) copy-start(f32[1000,320]{0,1:T(8,128)} %param.12) | copy-start | bytes 3840004
  1.3 1.1 %copy-start.1 = (bf16[3,320,320]{2,1,0:T(8,128)(2,1)S(1)}, bf16[3,320,320]{2,1,0:T(8,128)(2,1)}, u32[]{:S(2)}) copy-start(bf16[3,320,320]{2,1,0:T(8,128)(2,1)} %temporal_ref.1) | copy-start | bytes 1843204
  2.4 1.0 %copy-start.2 = (f32[4,4,16,512]{3,2,1,0:T(8,128)S(1)}, f32[4,4,16,512]{3,2,1,0:T(8,128)}, u32[]{:S(2)}) copy-start(f32[4,4,16,512]{3,2,1,0:T(8,128)} %states_ref.1) | copy-start | bytes 1572868
  3.5 0.9 %copy-start.3 = (bf16[320,144]{0,1:T(8,128)(2,1)S(1)}, bf16[320,144]{0,1:T(8,128)(2,1)}, u32[]{:S(2)}) copy-start(bf16[320,144]{0,1:T(8,128)(2,1)} %param.9) | copy-start | bytes 276484
  4.4 0.7 %copy-start.4 = (bf16[16,320]{1,0:T(8,128)(2,1)S(1)}, bf16[16,320]{1,0:T(8,128)(2,1)}, u32[]{:S(2)}) copy-start(bf16[16,320]{1,0:T(8,128)(2,1)} %out_weight_ref.1) | copy-start | bytes 30724
  5.1 0.7 %copy-start.5 = (f32[1000]{0:T(1024)S(1)}, f32[1000]{0:T(1024)}, u32[]{:S(2)}) copy-start(f32[1000]{0:T(1024)} %step_ref.1) | copy-start | bytes 12004
  5.8 0.7 %copy-start.6 = (s32[24]{0:T(128)S(1)}, s32[24]{0:T(128)}, u32[]{:S(2)}) copy-start(s32[24]{0:T(128)} %index_ref.1) | copy-start | bytes 292
  6.4 0.7 %copy-start.7 = (s32[2]{0:T(128)S(1)}, s32[2]{0:T(128)}, u32[]{:S(2)}) copy-start(s32[2]{0:T(128)} %slides_ref.1) | copy-start | bytes 28
